TPU v7x, 1024 devices: a whole 4x8x16 slice. The times are simulated.
1024 devices in a mesh: dp: 128 (over y, z), seq: 8 (over x, core).
Axes of the slice: x: 4, y: 8, z: 16, core: 2. Of those that a mesh axis runs over, the one named last changes fastest.
Arguments:
- section_input: bfloat16 [128, 1024, 1536], P('dp', 'seq'), may hold values from -6 to 6
- lengths: int32 [128], P('dp'), may hold values from 256 to 1024
- depthwise_taps_matrix: float32 [5, 1536], replicated, may hold values from -2.5 to 2.5
- depth_bias: float32 [1536], replicated, may hold values from -3 to 3
- norm_gain: float32 [1536], replicated, may hold values from 0.5 to 1.5
- proj_weight: bfloat16 [768, 1536], replicated, may hold values from -0.15625 to 0.15625
- proj_cotangent: bfloat16 [128, 1024, 768], P('dp', 'seq'), may hold values from -24 to 24
- skip_cotangent: bfloat16 [128, 1024, 1536], P('dp', 'seq'), may hold values from -6 to 6
Outputs:
- input_grad: bfloat16 [128, 1024, 1536], P('dp', 'seq')
- proj_grad: float32 [768, 1536], P('dp', 'seq')
- kernel_grad: float32 [5, 1536], replicated
- bias_grad: float32 [1536], replicated
- gain_grad: float32 [1536], replicated
All inputs are finite; a program needn't handle non-finite values.
Results may differ from a plain program's by a relative error of at most 0.0055.
Values may be sent and summed in bfloat16 or wider, within the bound.
A program may use at most 32 MiB of HBM per device.

v0:
```python
import jax
import jax.numpy as jnp
from jax import lax
from jax.sharding import PartitionSpec as P

DILATION_STEP = 4


def padded(cells, sides, width):
    for axis, dim in sides:
        count = lax.axis_size(axis)
        ends = count - 1
        head = lax.slice_in_dim(cells, 0, width, axis=dim)
        tail = lax.slice_in_dim(cells, cells.shape[dim] - width, cells.shape[dim], axis=dim)
        cells = jnp.concatenate(
            [
                lax.ppermute(tail, axis, [(i, (i + 1) % count) for i in range(ends)]),
                cells,
                lax.ppermute(head, axis, [((i + 1) % count, i) for i in range(ends)]),
            ],
            axis=dim,
        )
    return cells


def norm_gelu(hidden_state, norm_gain):
    inverse = lax.rsqrt(jnp.mean(hidden_state * hidden_state, axis=-1, keepdims=True) + 1e-06)
    return jax.nn.gelu(hidden_state * inverse * norm_gain)


def shards(
    section_input,
    lengths,
    depthwise_taps_matrix,
    depth_bias,
    norm_gain,
    proj_weight,
    proj_cotangent,
    skip_cotangent,
):
    samp_count = section_input.shape[0]
    position_count = section_input.shape[1]
    channels = section_input.shape[2]
    outputs = proj_cotangent.shape[2]
    kernel_taps = depthwise_taps_matrix.shape[0]
    receptive_reach = kernel_taps // 2 * DILATION_STEP
    positions = lax.axis_index("seq") * position_count + jnp.arange(position_count, dtype=jnp.int32)
    keep = (positions[None, :] < lengths[:, None]).astype(jnp.bfloat16)[:, :, None]
    masked = section_input * keep
    padded_input = padded(masked, (("seq", 1),), receptive_reach)
    hidden_state = jnp.zeros((samp_count, position_count, channels), jnp.float32) + depth_bias
    for kernel_tap in range(kernel_taps):
        hidden_state = hidden_state + depthwise_taps_matrix[kernel_tap] * padded_input[
            :, kernel_tap * DILATION_STEP : kernel_tap * DILATION_STEP + position_count
        ].astype(jnp.float32)
    activ, pull = jax.vjp(norm_gelu, hidden_state, norm_gain)
    activ_b = activ.astype(jnp.bfloat16)
    cot_rows = proj_cotangent.reshape(samp_count * position_count, outputs)
    back = jnp.dot(cot_rows, proj_weight, preferred_element_type=jnp.float32).reshape(
        samp_count, position_count, channels
    )
    back = back + skip_cotangent.astype(jnp.float32)
    hidden_grad, gain_part = pull(back)
    grad_b = hidden_grad.astype(jnp.bfloat16)
    grad_pad = padded(grad_b, (("seq", 1),), receptive_reach)
    input_grad = jnp.zeros((samp_count, position_count, channels), jnp.float32)
    for kernel_tap in range(kernel_taps):
        shift_offset = (kernel_taps - 1 - kernel_tap) * DILATION_STEP
        input_grad = input_grad + depthwise_taps_matrix[kernel_tap] * grad_pad[
            :, shift_offset : shift_offset + position_count
        ].astype(jnp.float32)
    input_grad = (input_grad * keep.astype(jnp.float32)).astype(jnp.bfloat16)
    gradient_function = grad_b.astype(jnp.float32)
    kernel_partial = jnp.stack(
        [
            jnp.sum(
                padded_input[
                    :, kernel_tap * DILATION_STEP : kernel_tap * DILATION_STEP + position_count
                ].astype(jnp.float32)
                * gradient_function,
                axis=(0, 1),
            )
            for kernel_tap in range(kernel_taps)
        ]
    )
    bias_part = jnp.sum(gradient_function, axis=(0, 1))
    kernel_sum, bias_sum, gain_sum = lax.psum((kernel_partial, bias_part, gain_part), ("dp", "seq"))
    samples_all = samp_count * lax.axis_size("dp")
    activ_cols = lax.all_to_all(activ_b, "seq", split_axis=2, concat_axis=1, tiled=True)
    col_count = activ_cols.shape[2]
    cot_whole = lax.all_gather(proj_cotangent, "seq", axis=1, tiled=True)
    cot_flat = cot_whole.reshape(-1, outputs)
    act_flat = activ_cols.reshape(-1, col_count)
    proj_sum = lax.psum_scatter(
        lax.dot_general(
            cot_flat, act_flat, (((0,), (0,)), ((), ())), preferred_element_type=jnp.float32
        ),
        "dp",
        scatter_dimension=0,
        tiled=True,
    )
    return (
        input_grad,
        proj_sum / samples_all,
        kernel_sum / samples_all,
        bias_sum / samples_all,
        gain_sum / samples_all,
    )


def solution(mesh):
    in_specs = (
        P("dp", "seq", None),
        P("dp"),
        P(),
        P(),
        P(),
        P(),
        P("dp", "seq", None),
        P("dp", "seq", None),
    )
    out_specs = (P("dp", "seq", None), P("dp", "seq"), P(), P(), P())
    return jax.shard_map(shards, mesh=mesh, in_specs=in_specs, out_specs=out_specs, check_vma=False)
```

profile of v0, /device:TPU:4, one launch (start us, length us, event | category | flops | bytes accessed | tf_op | source)
XLA Modules:
  0.0 469.2 jit_solution(4183135703973376379)
XLA Ops:
  7.3 0.7 all-gather.2.cloned.1.call-update
  9.3 1.1 broadcast_multiply_fusion
  10.4 1.9 collective-permute-start
  12.3 3.6 collective-permute-start.1
  16.0 1.1 slice_reduce_fusion.4
  17.1 1.3 dynamic-slice
  19.0 1.2 multiply_reduce_fusion.2
  20.3 1.7 multiply_reduce_fusion
  22.0 2.3 fusion.27
  27.2 2.2 copy.17
  29.9 9.5 %reduce.13 = bf16[1536,128]{1,0:T(8,128)(2,1)} reduce(bf16[1536,1,128]{2,1,0:T(2,128)(2,1)S(1)} %bitcast.36, bf16[]{:T(256)} %broadcast.111), dimensions={1}, to_apply=%bitcast.30.reduce_sub_computation | reduce | bytes 786434
  39.4 1.9 reshape.111
  41.3 14.2 %all-to-all-start = ((bf16[8,2,12288]{2,1,0:T(2,128)(2,1)}), bf16[8,2,12288]{2,1,0:T(2,128)(2,1)}, u32[]{:S(2)}, u32[]{:S(2)}) async-start(bf16[8,2,12288]{2,1,0:T(2,128)(2,1)} %reshape.111), calls=%async_computation | async-start | bytes 786432 | tf_op jit(solution)/shard_map/all_to_all | solution.py:89
  56.1 2.2 collective-permute-start.2
  58.3 2.1 collective-permute-start.3
  60.4 0.8 stack.23
  61.2 126.0 %all-reduce.1 = (f32[5,1536]{1,0:T(8,128)S(1)}, f32[1536]{0:T(1024)}, f32[1536]{0:T(1024)}) all-reduce(f32[5,1536]{1,0:T(8,128)S(1)} %stack.23, f32[1536]{0:T(1024)} %get-tuple-element.29, f32[1536]{0:T(1024)} %get-tuple-element.20), channel_id=1, replica_groups=mesh['dp'=128,'seq'=8] {'dp','seq'}, use_global_device_ids=true, to_apply=%region_8.0 | all-reduce | flops 10752 | bytes 86016 | tf_op jit(solution)/shard_map/psum | solution.py:87
  187.2 0.6 broadcast_multiply_fusion.1
  187.8 2.6 reshape.112
  190.9 2.7 fusion.3
  194.3 1.9 fusion.22
  196.2 264.4 %all-reduce.4.cloned.1.call-done = f32[768,192]{0,1:T(8,128)} async-done(((f32[768,192]{0,1:T(8,128)}), f32[768,192]{0,1:T(8,128)}) %all-reduce.4.cloned.1.call-update) | async-done | bytes 589840
  460.6 1.0 dynamic-slice_multiply_fusion
  461.7 0.7 copy.19
  (49 shorter events, 5.8 us)
Async XLA Ops:
  7.2 13.1 %copy-start = (bf16[768,1536]{1,0:T(8,128)(2,1)S(1)}, bf16[768,1536]{1,0:T(8,128)(2,1)}, u32[]{:S(2)}) copy-start(bf16[768,1536]{1,0:T(8,128)(2,1)} %param.13) | copy-start | bytes 7077892
  7.2 13.1 %copy-start.1 = (bf16[1,128,768]{2,1,0:T(8,128)(2,1)S(1)}, bf16[1,128,768]{2,1,0:T(8,128)(2,1)}, u32[]{:S(2)}) copy-start(bf16[1,128,768]{2,1,0:T(8,128)(2,1)} %param.14) | copy-start | bytes 589828
  7.2 13.1 %copy-start.8 = (f32[1536]{0:T(1024)S(1)}, f32[1536]{0:T(1024)}, u32[]{:S(2)}) copy-start(f32[1536]{0:T(1024)} %param.12) | copy-start | bytes 18436
  7.2 13.1 %copy-start.12 = (bf16[1,128,1536]{2,1,0:T(8,128)(2,1)S(1)}, bf16[1,128,1536]{2,1,0:T(8,128)(2,1)}, u32[]{:S(2)}) copy-start(bf16[1,128,1536]{2,1,0:T(8,128)(2,1)} %param.15) | copy-start | bytes 1179652
  7.2 183.7 %all-gather.2.cloned.1.call-start = ((), (), s32[]{:S(2)}) async-start(), calls=%async_computation.1 | async-start | bytes 1769472 | tf_op jit(solution)/shard_map/all_gather | solution.py:91
  10.4 8.6 %collective-permute-start = (bf16[1,8,1536]{2,1,0:T(8,128)(2,1)S(1)}, bf16[1,8,1536]{2,1,0:T(8,128)(2,1)S(1)}, u32[]{:S(2)}, u32[]{:S(2)}) collective-permute-start(bf16[1,8,1536]{2,1,0:T(8,128)(2,1)S(1)} %get-tuple-element.46), channel_id=1, source_target_pairs={{0,1},{1,2},{2,3},{3,4},{4,5},{5,6},{6,7},{8,9},{9,10},{10,11},{11... | collective-permute-start | bytes 73736 | tf_op jit(solution)/shard_map/ppermute | solution.py:17
  12.3 6.7 %collective-permute-start.1 = (bf16[1,8,1536]{2,1,0:T(8,128)(2,1)S(1)}, bf16[1,8,1536]{2,1,0:T(8,128)(2,1)S(1)}, u32[]{:S(2)}, u32[]{:S(2)}) collective-permute-start(bf16[1,8,1536]{2,1,0:T(8,128)(2,1)S(1)} %get-tuple-element.47), channel_id=1, source_target_pairs={{1,0},{2,1},{3,2},{4,3},{5,4},{6,5},{7,6},{9,8},{10,9},{11,10},{12... | collective-permute-start | bytes 73736 | tf_op jit(solution)/shard_map/ppermute | solution.py:19
  17.1 4.9 %copy-start.2 = (f32[1536]{0:T(1024)}, f32[1536]{0:T(1024)S(1)}, u32[]{:S(2)}) copy-start(f32[1536]{0:T(1024)S(1)} %get-tuple-element.32) | copy-start | bytes 18436
  17.1 4.9 %copy-start.4 = (f32[1536]{0:T(1024)}, f32[1536]{0:T(1024)S(1)}, u32[]{:S(2)}) copy-start(f32[1536]{0:T(1024)S(1)} %get-tuple-element.33) | copy-start | bytes 18436
  17.1 4.9 %copy-start.6 = (f32[1536]{0:T(1024)}, f32[1536]{0:T(1024)S(1)}, u32[]{:S(2)}) copy-start(f32[1536]{0:T(1024)S(1)} %get-tuple-element.34) | copy-start | bytes 18436
  41.3 146.6 %all-to-all-start = ((bf16[8,2,12288]{2,1,0:T(2,128)(2,1)}), bf16[8,2,12288]{2,1,0:T(2,128)(2,1)}, u32[]{:S(2)}, u32[]{:S(2)}) async-start(bf16[8,2,12288]{2,1,0:T(2,128)(2,1)} %reshape.111), calls=%async_computation | async-start | bytes 786432 | tf_op jit(solution)/shard_map/all_to_all | solution.py:89
  55.4 405.2 %all-reduce.4.cloned.1.call-start = ((), (), s32[]{:S(2)}) async-start(), calls=%async_computation.2 | async-start | bytes 1179648
  56.1 138.2 %collective-permute-start.2 = (bf16[1,8,1536]{2,1,0:T(8,128)(2,1)}, bf16[1,8,1536]{2,1,0:T(8,128)(2,1)}, u32[]{:S(2)}, u32[]{:S(2)}) collective-permute-start(bf16[1,8,1536]{2,1,0:T(8,128)(2,1)} %get-tuple-element.44), channel_id=1, source_target_pairs={{1,0},{2,1},{3,2},{4,3},{5,4},{6,5},{7,6},{9,8},{10,9},{11,10},{12... | collective-permute-start | bytes 73736 | tf_op jit(solution)/shard_map/ppermute | solution.py:19
  58.3 136.0 %collective-permute-start.3 = (bf16[1,8,1536]{2,1,0:T(8,128)(2,1)}, bf16[1,8,1536]{2,1,0:T(8,128)(2,1)}, u32[]{:S(2)}, u32[]{:S(2)}) collective-permute-start(bf16[1,8,1536]{2,1,0:T(8,128)(2,1)} %get-tuple-element.45), channel_id=1, source_target_pairs={{0,1},{1,2},{2,3},{3,4},{4,5},{5,6},{6,7},{8,9},{9,10},{10,11},{11... | collective-permute-start | bytes 73736 | tf_op jit(solution)/shard_map/ppermute | solution.py:17
  190.5 3.1 copy-start.9
  190.5 3.1 copy-start.10
  190.5 3.7 copy-start.3
  190.5 3.7 copy-start.5
  190.6 3.7 copy-start.7
  190.6 3.7 copy-start.11
Sparse Core Ops, SparseCore 0:
  10.8 41.6 all-gather.1
  193.7 266.8 all-reduce.3
where the time goes:
time: 470 us; the launch traced here: 469 us
  waiting for transfers between devices  265 us (56%)
  blocking collectives  126 us (27%)
  starting transfers between devices  24.1 us (5%)
  other arithmetic  18.8 us (4%)
  between operations  15.8 us (3%)
  local copies, waits for them, and re-layouts  15 us (3%)
    unnamed x3, waiting for transfers between devices  265 us
    psum x1, blocking collectives, shards(): lax.psum((kernel_partial, bias_part, gain_part), ('dp', 'seq'))  126 us
    all_to_all x1, starting transfers between devices, shards(): lax.all_to_all(activ_b, 'seq', split_axis=2, concat_axis=1, tiled=True)  14.2 us
    unnamed x1, other arithmetic  9.51 us
  transfers between devices with their start and end apart: 7, of which 1 were waited for; matrix products, arithmetic and copies ran while one was open for 8% of the time, Pallas kernels for 0%

commit v1 on v0

v1 whole, which is shorter than its diff:
```python
import functools

import jax
import jax.numpy as jnp
from jax import lax
from jax.experimental import pallas as pl
from jax.experimental.pallas import tpu as pltpu
from jax.sharding import PartitionSpec as P

STEP = 4
MESH = pl.DeviceIdType.MESH
BLOCK = 16
HALO = 8
XS = 4
LANES = 128
ROOT = 0.7978845608028654
CUBIC = 0.044715

LOC_X, LOC_COT, LOC_SKIP, LOC_W, LOC_OWN, LOC_ACT = range(6)
(S_HALO, S_COT, S_ACT, S_SIB, S_GRAD, S_EX, S_EY, S_EZ, S_EA, S_EF, S_PY, S_PZ) = range(12)
(R_TOP, R_BOT, R_COT, R_ACT1, R_ACT2, R_ACT3, R_SIB, R_GTOP, R_GBOT, R_EX, R_EY, R_EZ, R_EA, R_EF, R_PY, R_PZ) = range(16)


def wait_bytes(ref, sem):
    pltpu.make_async_copy(ref, ref, sem).wait()


def kernel(
    ys,
    zs,
    len_ref,
    x_hbm,
    cot_hbm,
    skip_hbm,
    w_hbm,
    taps_ref,
    bias_ref,
    gain_ref,
    ig_ref,
    pg_ref,
    kg_ref,
    bg_ref,
    gg_ref,
    x_v,
    cot_v,
    skip_v,
    w_v,
    back,
    halo_t,
    halo_b,
    xpad,
    gb,
    ghalo_t,
    ghalo_b,
    gpad,
    eacc,
    cotg,
    actc,
    actg,
    pacc,
    pbuf,
    yrecv,
    tbuf,
    zrecv,
    e_loc,
    e_x,
    e_1,
    e_y,
    e_z,
    e_fin,
    loc,
    snd,
    rcv,
):
    rows, chans = x_v.shape
    outs = cot_v.shape[1]
    half = outs // 2
    quarter = chans // XS
    taps = taps_ref.shape[0]
    samples = ys * zs
    own_rows = outs // samples
    yh, zh = ys // 2, zs // 2
    k_rows = own_rows * zh
    tile = tbuf.shape[2]
    e_rows = e_1.shape[1]

    dp = lax.axis_index("dp")
    s = lax.axis_index("seq")
    y, z = dp // zs, dp % zs
    x, c = s // 2, s % 2
    oc = 1 - c
    sib = 2 * x + oc

    def xat(delta, core):
        return (dp, 2 * ((x + delta) % XS) + core)

    def remote(src, dst, send, recv, device):
        return pltpu.make_async_remote_copy(
            src_ref=src, dst_ref=dst, send_sem=snd.at[send], recv_sem=rcv.at[recv], device_id=device, device_id_type=MESH
        )

    ld_x = pltpu.make_async_copy(x_hbm, x_v, loc.at[LOC_X])
    ld_cot = pltpu.make_async_copy(cot_hbm, cot_v, loc.at[LOC_COT])
    ld_w = pltpu.make_async_copy(w_hbm, w_v, loc.at[LOC_W])
    ld_skip = pltpu.make_async_copy(skip_hbm, skip_v, loc.at[LOC_SKIP])
    my_half = pl.multiple_of(c * half, LANES)
    ld_own = pltpu.make_async_copy(cot_hbm.at[:, pl.ds(my_half, half)], cotg.at[0], loc.at[LOC_OWN])
    ld_x.start()
    ld_cot.start()
    ld_w.start()
    ld_skip.start()
    ld_own.start()

    barrier = pltpu.get_barrier_semaphore()

    def greet(device):
        pl.semaphore_signal(barrier, inc=1, device_id=device, device_id_type=MESH)

    for d in range(1, 2 * XS):
        greet((dp, (s + d) % (2 * XS)))

    def greet_y(d, carry):
        other = ((y + d) % ys) * zs + z
        greet((other, s))
        greet((other, sib))
        return carry

    def greet_z(d, carry):
        other = y * zs + (z + d) % zs
        greet((other, s))
        greet((other, sib))
        return carry

    lax.fori_loop(1, ys, greet_y, 0)
    lax.fori_loop(1, zs, greet_z, 0)
    pl.semaphore_wait(barrier, 2 * XS - 1 + 2 * (ys - 1) + 2 * (zs - 1))

    up, down = (dp, (s + 1) % (2 * XS)), (dp, (s + 2 * XS - 1) % (2 * XS))
    remote(x_hbm.at[pl.ds(rows - BLOCK, BLOCK)], halo_t, S_HALO, R_TOP, up).start()
    remote(x_hbm.at[pl.ds(0, BLOCK)], halo_b, S_HALO, R_BOT, down).start()

    for delta in (1, 3, 2, 0):
        for p in (0, 1):
            if delta == 0 and p == 0:
                continue
            core = c if p == 0 else oc
            start = pl.multiple_of(core * half, LANES)
            remote(
                cot_hbm.at[:, pl.ds(start, half)], cotg.at[4 * p + (XS - delta) % XS], S_COT, R_COT, xat(delta, core)
            ).start()

    length = len_ref[0]
    first = s * rows
    row_id = lax.broadcasted_iota(jnp.int32, (BLOCK, 1), 0)

    ld_cot.wait()
    ld_w.wait()
    ld_skip.wait()

    def back_step(i, carry):
        at = pl.ds(pl.multiple_of(i * quarter, LANES), quarter)
        back[:, at] = jnp.dot(cot_v[...], w_v[:, at], preferred_element_type=jnp.float32) + skip_v[:, at].astype(jnp.float32)
        return carry

    lax.fori_loop(0, XS, back_step, 0)

    ld_x.wait()

    def mask_step(i, carry):
        r0 = pl.multiple_of(i * BLOCK, BLOCK)
        value = x_v[pl.ds(r0, BLOCK), :].astype(jnp.float32)
        xpad[pl.ds(r0 + HALO, BLOCK), :] = jnp.where(first + r0 + row_id < length, value, 0.0)
        return carry

    lax.fori_loop(0, rows // BLOCK, mask_step, 0)
    eacc[...] = jnp.zeros_like(eacc)

    wait_bytes(halo_t, rcv.at[R_TOP])
    wait_bytes(halo_b, rcv.at[R_BOT])
    head_id = first - HALO + lax.broadcasted_iota(jnp.int32, (HALO, 1), 0)
    head = halo_t[...].astype(jnp.float32)[BLOCK - HALO :]
    xpad[0:HALO, :] = jnp.where(jnp.logical_and(head_id >= 0, head_id < length), head, 0.0)
    tail_id = first + rows + lax.broadcasted_iota(jnp.int32, (HALO, 1), 0)
    tail = halo_b[...].astype(jnp.float32)[:HALO]
    xpad[pl.ds(rows + HALO, HALO), :] = jnp.where(
        jnp.logical_and(tail_id < length, s < 2 * XS - 1), tail, 0.0
    )

    def fold(value):
        return value[:HALO] + value[HALO:]

    def shifted(ref, r0):
        even = ref[pl.ds(r0, 2 * BLOCK), :]
        odd = even[STEP : STEP + BLOCK + HALO]
        return [even[:BLOCK], odd[:BLOCK], even[HALO : HALO + BLOCK], odd[HALO:], even[BLOCK:]]

    def main_step(i, carry):
        r0 = pl.multiple_of(i * BLOCK, BLOCK)
        seen = shifted(xpad, r0)
        hidden = bias_ref[...] + taps_ref[0:1, :] * seen[0]
        for j in range(1, taps):
            hidden = hidden + taps_ref[j : j + 1, :] * seen[j]
        inverse = lax.rsqrt(jnp.mean(hidden * hidden, axis=-1, keepdims=True) + 1e-06)
        normed = hidden * inverse
        gain = gain_ref[...]
        u = normed * gain
        square = u * u
        tanh = jnp.tanh(u * (ROOT + ROOT * CUBIC * square))
        cdf = 0.5 + 0.5 * tanh
        act = (u * cdf).astype(jnp.bfloat16)
        for q in range(XS):
            actc[q, pl.ds(r0, BLOCK), :] = act[:, q * quarter : (q + 1) * quarter]
        slope = cdf + u * (1.0 - tanh * tanh) * (0.5 * ROOT + 1.5 * ROOT * CUBIC * square)
        toward = back[pl.ds(r0, BLOCK), :] * slope
        eacc[pl.ds((taps + 1) * HALO, HALO), :] += fold(toward * normed)
        toward = toward * gain
        pull = jnp.mean(toward * normed, axis=-1, keepdims=True)
        grad = ((toward - normed * pull) * inverse).astype(jnp.bfloat16)
        gb[pl.ds(r0, BLOCK), :] = grad
        grad = grad.astype(jnp.float32)
        gpad[pl.ds(r0 + HALO, BLOCK), :] = grad
        eacc[pl.ds(taps * HALO, HALO), :] += fold(grad)
        for j in range(taps):
            eacc[pl.ds(j * HALO, HALO), :] += fold(grad * seen[j])
        return carry

    lax.fori_loop(0, rows // BLOCK, main_step, 0)

    for delta in (1, 3, 2):
        remote(
            actc.at[(x + delta) % XS], actg.at[XS - delta], S_ACT, R_ACT1 + (XS - delta) - 1, xat(delta, c)
        ).start()
    remote(actc.at[x], actg.at[4], S_SIB, R_SIB, (dp, sib)).start()
    own_act = pltpu.make_async_copy(actc.at[x], actg.at[0], loc.at[LOC_ACT])
    own_act.start()

    remote(gb.at[pl.ds(rows - BLOCK, BLOCK)], ghalo_t, S_GRAD, R_GTOP, up).start()
    remote(gb.at[pl.ds(0, BLOCK)], ghalo_b, S_GRAD, R_GBOT, down).start()

    for r in range(taps + 2):
        line = jnp.sum(eacc[r * HALO : (r + 1) * HALO, :], axis=0, keepdims=True)
        for q in range(XS):
            e_loc[q, r : r + 1, :] = line[:, q * quarter : (q + 1) * quarter]
    for q in range(XS):
        e_loc[q, taps + 2 :, :] = jnp.zeros((HALO - taps - 2, quarter), jnp.float32)
    for delta in (1, 3, 2):
        remote(e_loc.at[(x + delta) % XS], e_x.at[XS - delta - 1], S_EX, R_EX, xat(delta, c)).start()

    wait_bytes(ghalo_t, rcv.at[R_GTOP])
    wait_bytes(ghalo_b, rcv.at[R_GBOT])
    gpad[0:HALO, :] = jnp.where(s > 0, ghalo_t[...].astype(jnp.float32)[BLOCK - HALO :], 0.0)
    gpad[pl.ds(rows + HALO, HALO), :] = jnp.where(s < 2 * XS - 1, ghalo_b[...].astype(jnp.float32)[:HALO], 0.0)

    def input_step(i, carry):
        r0 = pl.multiple_of(i * BLOCK, BLOCK)
        seen = shifted(gpad, r0)
        total = taps_ref[0:1, :] * seen[taps - 1]
        for j in range(1, taps):
            total = total + taps_ref[j : j + 1, :] * seen[taps - 1 - j]
        ig_ref[pl.ds(r0, BLOCK), :] = jnp.where(first + r0 + row_id < length, total, 0.0).astype(jnp.bfloat16)
        return carry

    lax.fori_loop(0, rows // BLOCK, input_step, 0)

    wait_bytes(e_x, rcv.at[R_EX])
    e_sum = e_loc[x] + e_x[0] + e_x[1] + e_x[2]
    for r in range(HALO):
        e_1[r // e_rows, r % e_rows : r % e_rows + 1, :] = e_sum[r : r + 1]
    for d in range(1, ys):
        other = (y + d) % ys
        remote(e_1.at[other], e_y.at[ys - d - 1], S_EY, R_EY, (other * zs + z, s)).start()

    wait_bytes(cotg.at[pl.ds(1, 7)], rcv.at[R_COT])
    ld_own.wait()
    for d in (3, 1, 2):
        wait_bytes(actg.at[d], rcv.at[R_ACT1 + d - 1])
        remote(actg.at[d], actg.at[4 + d], S_SIB, R_SIB, (dp, sib)).start()
    own_act.wait()

    def product(at):
        a = cotg[at : at + 4].reshape(4 * rows, half)
        b = actg[at : at + 4].reshape(4 * rows, quarter)
        return lax.dot_general(a, b, (((0,), (0,)), ((), ())), preferred_element_type=jnp.float32)

    pacc[...] = product(0)

    wait_bytes(e_y, rcv.at[R_EY])
    e_row = e_1[y]
    for d in range(ys - 1):
        e_row = e_row + e_y[d]
    e_z[z] = e_row
    for d in range(1, zs):
        remote(e_z.at[z], e_z.at[z], S_EZ, R_EZ, (y * zs + (z + d) % zs, s)).start()

    wait_bytes(actg.at[pl.ds(4, 4)], rcv.at[R_SIB])
    part = (pacc[...] + product(4)).astype(jnp.bfloat16)
    for i in range(ys):
        pbuf[i] = part[i * k_rows : (i + 1) * k_rows]

    for i in range(yh):
        for k in range(2):
            other = yh * c + i
            slot = (y + ys - other) % ys
            mine = jnp.logical_and(other == y, c == k)

            @pl.when(mine)
            def _():
                yrecv[0] = pbuf[2 * i + k]

            @pl.when(jnp.logical_not(mine))
            def _():
                remote(pbuf.at[2 * i + k], yrecv.at[slot], S_PY, R_PY, (other * zs + z, 2 * x + k)).start()

    wait_bytes(e_z.at[pl.ds(0, zs - 1)], rcv.at[R_EZ])
    e_row = e_z[0]
    for d in range(1, zs):
        e_row = e_row + e_z[d]
    e_fin[s, y] = e_row
    for d in range(1, ys):
        remote(e_fin.at[s, y], e_fin.at[s, y], S_EA, R_EA, (((y + d) % ys) * zs + z, s)).start()

    own_y = y // yh == c

    @pl.when(own_y)
    def _():
        wait_bytes(yrecv.at[pl.ds(0, ys - 1)], rcv.at[R_PY])

    @pl.when(jnp.logical_not(own_y))
    def _():
        wait_bytes(yrecv, rcv.at[R_PY])

    total = yrecv[0].astype(jnp.float32)
    for d in range(1, ys):
        total = total + yrecv[d].astype(jnp.float32)
    total = total.astype(jnp.bfloat16)
    sel_row = lax.broadcasted_iota(jnp.int32, (zh * tile, k_rows), 0)
    sel_col = lax.broadcasted_iota(jnp.int32, (zh * tile, k_rows), 1)
    within = sel_row % tile
    base = (sel_row // tile) * own_rows
    pick_a = jnp.logical_and(within < own_rows, sel_col == base + within).astype(jnp.bfloat16)
    low = within - tile // 2
    pick_b = jnp.logical_and(jnp.logical_and(low >= 0, low < own_rows), sel_col == base + low).astype(jnp.bfloat16)
    middle = jnp.dot(pick_b, total[:, LANES : 2 * LANES], preferred_element_type=jnp.float32)
    for q in range(2):
        outer = jnp.dot(pick_a, total[:, 2 * LANES * q : 2 * LANES * q + LANES], preferred_element_type=jnp.float32)
        both = (outer + middle).astype(jnp.bfloat16)
        for j in range(zh):
            tbuf[j, q] = both[j * tile : (j + 1) * tile]
    for j in range(zh):
        for q in range(2):
            other = zh * c + j
            slot = (z + zs - other) % zs
            mine = jnp.logical_and(other == z, c == q)

            @pl.when(mine)
            def _():
                zrecv[0] = tbuf[j, q]

            @pl.when(jnp.logical_not(mine))
            def _():
                remote(tbuf.at[j, q], zrecv.at[slot], S_PZ, R_PZ, (y * zs + other, 2 * x + q)).start()

    wait_bytes(e_fin.at[0, pl.ds(0, ys - 1)], rcv.at[R_EA])
    for d in range(1, 2 * XS):
        remote(e_fin.at[s], e_fin.at[s], S_EF, R_EF, (dp, (s + d) % (2 * XS))).start()

    own_z = z // zh == c

    @pl.when(own_z)
    def _():
        wait_bytes(zrecv.at[pl.ds(0, zs - 1)], rcv.at[R_PZ])

    @pl.when(jnp.logical_not(own_z))
    def _():
        wait_bytes(zrecv, rcv.at[R_PZ])

    final = zrecv[0].astype(jnp.float32)
    for d in range(1, zs):
        final = final + zrecv[d].astype(jnp.float32)
    final = final / samples
    side = final[:own_rows]
    inner = final[tile // 2 : tile // 2 + own_rows]
    cut = quarter // 2 - LANES
    first_half = jnp.concatenate([side, inner[:, :cut]], axis=1)
    second_half = jnp.concatenate([inner[:, cut:], side], axis=1)
    pg_ref[...] = jnp.where(c == 0, first_half, second_half)

    wait_bytes(e_fin.at[pl.ds(0, 2 * XS - 1)], rcv.at[R_EF])
    for q in range(XS):
        at = slice(q * quarter, (q + 1) * quarter)
        for r in range(taps + 2):
            line = (e_fin[2 * q, r // e_rows, r % e_rows : r % e_rows + 1] + e_fin[2 * q + 1, r // e_rows, r % e_rows : r % e_rows + 1]) / samples
            if r < taps:
                kg_ref[r : r + 1, at] = line
            elif r == taps:
                bg_ref[:, at] = line
            else:
                gg_ref[:, at] = line

    wait_bytes(x_v.at[pl.ds(0, 2 * BLOCK)], snd.at[S_HALO])
    wait_bytes(cotg.at[pl.ds(0, 7)], snd.at[S_COT])
    wait_bytes(actg.at[pl.ds(0, 3)], snd.at[S_ACT])
    wait_bytes(actg.at[pl.ds(0, 4)], snd.at[S_SIB])
    wait_bytes(gb.at[pl.ds(0, 2 * BLOCK)], snd.at[S_GRAD])
    wait_bytes(e_x, snd.at[S_EX])
    wait_bytes(e_y, snd.at[S_EY])
    wait_bytes(e_z.at[pl.ds(0, zs - 1)], snd.at[S_EZ])
    wait_bytes(e_fin.at[0, pl.ds(0, ys - 1)], snd.at[S_EA])
    wait_bytes(e_fin.at[pl.ds(0, 2 * XS - 1)], snd.at[S_EF])

    @pl.when(own_y)
    def _():
        wait_bytes(pbuf.at[pl.ds(0, ys - 1)], snd.at[S_PY])

    @pl.when(jnp.logical_not(own_y))
    def _():
        wait_bytes(pbuf, snd.at[S_PY])

    @pl.when(own_z)
    def _():
        wait_bytes(zrecv.at[pl.ds(0, zs - 1)], snd.at[S_PZ])

    @pl.when(jnp.logical_not(own_z))
    def _():
        wait_bytes(zrecv, snd.at[S_PZ])


def shards(ys, zs, section, lengths, taps, bias, gain, weight, cot, skip):
    samp, rows, chans = section.shape
    outs = cot.shape[2]
    half, quarter = outs // 2, chans // XS
    samples = ys * zs
    own_rows = outs // samples
    k_rows = own_rows * (zs // 2)
    tile = 2 * (-(-own_rows // 8) * 8)
    e_rows = HALO // ys
    kinds = taps.shape[0]
    bf16, f32 = jnp.bfloat16, jnp.float32
    vmem = pl.BlockSpec(memory_space=pltpu.VMEM)
    anywhere = pl.BlockSpec(memory_space=pl.ANY)
    result = pl.pallas_call(
        functools.partial(kernel, ys, zs),
        out_shape=(
            jax.ShapeDtypeStruct((rows, chans), bf16),
            jax.ShapeDtypeStruct((own_rows, quarter // 2), f32),
            jax.ShapeDtypeStruct((kinds, chans), f32),
            jax.ShapeDtypeStruct((1, chans), f32),
            jax.ShapeDtypeStruct((1, chans), f32),
        ),
        in_specs=[pl.BlockSpec(memory_space=pltpu.SMEM), anywhere, anywhere, anywhere, anywhere, vmem, vmem, vmem],
        out_specs=(vmem,) * 5,
        scratch_shapes=[
            pltpu.VMEM((rows, chans), bf16),
            pltpu.VMEM((rows, outs), bf16),
            pltpu.VMEM((rows, chans), bf16),
            pltpu.VMEM((outs, chans), bf16),
            pltpu.VMEM((rows, chans), f32),
            pltpu.VMEM((BLOCK, chans), bf16),
            pltpu.VMEM((BLOCK, chans), bf16),
            pltpu.VMEM((rows + 2 * HALO, chans), f32),
            pltpu.VMEM((rows, chans), bf16),
            pltpu.VMEM((BLOCK, chans), bf16),
            pltpu.VMEM((BLOCK, chans), bf16),
            pltpu.VMEM((rows + 2 * HALO, chans), f32),
            pltpu.VMEM(((kinds + 2) * HALO, chans), f32),
            pltpu.VMEM((8, rows, half), bf16),
            pltpu.VMEM((XS, rows, quarter), bf16),
            pltpu.VMEM((8, rows, quarter), bf16),
            pltpu.VMEM((half, quarter), f32),
            pltpu.VMEM((ys, k_rows, quarter), bf16),
            pltpu.VMEM((ys, k_rows, quarter), bf16),
            pltpu.VMEM((zs // 2, 2, tile, LANES), bf16),
            pltpu.VMEM((zs, tile, LANES), bf16),
            pltpu.VMEM((XS, HALO, quarter), f32),
            pltpu.VMEM((XS - 1, HALO, quarter), f32),
            pltpu.VMEM((ys, e_rows, quarter), f32),
            pltpu.VMEM((ys - 1, e_rows, quarter), f32),
            pltpu.VMEM((zs, e_rows, quarter), f32),
            pltpu.VMEM((2 * XS, ys, e_rows, quarter), f32),
            pltpu.SemaphoreType.DMA((6,)),
            pltpu.SemaphoreType.DMA((12,)),
            pltpu.SemaphoreType.DMA((16,)),
        ],
        compiler_params=pltpu.CompilerParams(collective_id=0, has_side_effects=True, vmem_limit_bytes=48 * 1024 * 1024),
        cost_estimate=pl.CostEstimate(flops=4 * rows * outs * chans, bytes_accessed=4_000_000, transcendentals=rows * chans),
    )(
        lengths,
        section.reshape(rows, chans),
        cot.reshape(rows, outs),
        skip.reshape(rows, chans),
        weight,
        taps,
        bias.reshape(1, chans),
        gain.reshape(1, chans),
    )
    input_grad, proj, taps_grad, bias_grad, gain_grad = result
    return input_grad.reshape(section.shape), proj, taps_grad, bias_grad.reshape(chans), gain_grad.reshape(chans)


def solution(mesh):
    dp = mesh.shape["dp"]
    ys = 8 if dp == 128 else 2
    in_specs = (
        P("dp", "seq", None),
        P("dp"),
        P(),
        P(),
        P(),
        P(),
        P("dp", "seq", None),
        P("dp", "seq", None),
    )
    out_specs = (P("dp", "seq", None), P("dp", "seq"), P(), P(), P())
    return jax.shard_map(
        functools.partial(shards, ys, dp // ys), mesh=mesh, in_specs=in_specs, out_specs=out_specs, check_vma=False
    )
```

time: 470 us -> 75.3 us (0.16)
  the two profiles are of different devices: /device:TPU:4 before, /device:TPU:9 now
where the time goes in v1:
time: 75.3 us; the launch traced here: 74.9 us
  Pallas kernels  63.6 us (84%)
  local copies, waits for them, and re-layouts  8.75 us (12%)
  between operations  1.29 us (2%)
  other arithmetic  1.24 us (2%)
    pallas_call x1, Pallas kernels, shards(): pl.pallas_call(functools.partial(kernel, ys, zs), out_shape=(jax.ShapeDty...  63.6 us
    unnamed x13, local copies, waits for them, and re-layouts  7.34 us

profile of v1, /device:TPU:9, one launch (start us, length us, event | category | flops | bytes accessed | tf_op | source)
XLA Modules:
  0.0 74.9 jit_solution(10861936012661857486)
XLA Ops:
  1.3 0.7 reshape.37.bias_ref
  2.0 0.7 reshape.38.gain_ref
  2.7 0.0 copy-start
  2.7 1.7 %copy-done = bf16[768,1536]{1,0:T(8,128)(2,1)S(1)} copy-done((bf16[768,1536]{1,0:T(8,128)(2,1)S(1)}, bf16[768,1536]{1,0:T(8,128)(2,1)}, u32[]{:S(2)}) %copy-start) | copy-done | bytes 2359320
  4.3 0.0 copy-start.1
  4.3 1.0 %copy-done.1 = bf16[1,128,1536]{2,1,0:T(8,128)(2,1)S(1)} copy-done((bf16[1,128,1536]{2,1,0:T(8,128)(2,1)S(1)}, bf16[1,128,1536]{2,1,0:T(8,128)(2,1)}, u32[]{:S(2)}) %copy-start.1) | copy-done | bytes 393240
  5.3 0.0 copy-start.2
  5.3 1.0 %copy-done.2 = bf16[1,128,1536]{2,1,0:T(8,128)(2,1)S(1)} copy-done((bf16[1,128,1536]{2,1,0:T(8,128)(2,1)S(1)}, bf16[1,128,1536]{2,1,0:T(8,128)(2,1)}, u32[]{:S(2)}) %copy-start.2) | copy-done | bytes 393240
  6.3 0.0 copy-start.3
  6.3 0.9 %copy-done.3 = bf16[1,128,768]{2,1,0:T(8,128)(2,1)S(1)} copy-done((bf16[1,128,768]{2,1,0:T(8,128)(2,1)S(1)}, bf16[1,128,768]{2,1,0:T(8,128)(2,1)}, u32[]{:S(2)}) %copy-start.3) | copy-done | bytes 196632
  7.3 0.0 copy-start.4
  7.3 0.8 %copy-done.4 = f32[5,1536]{1,0:T(8,128)S(1)} copy-done((f32[5,1536]{1,0:T(8,128)S(1)}, f32[5,1536]{1,0:T(8,128)}, u32[]{:S(2)}) %copy-start.4) | copy-done | bytes 30744
  8.1 63.6 %shard_map.119 = (bf16[128,1536]{1,0:T(8,128)(2,1)S(1)}, f32[6,192]{1,0:T(8,128)S(1)}, f32[5,1536]{1,0:T(8,128)S(1)}, f32[1,1536]{1,0:T(1,128)S(1)}, f32[1,1536]{1,0:T(1,128)S(1)}) custom-call(s32[1]{0:T(128)S(6)} %copy.16.len_ref, bf16[128,1536]{1,0:T(8,128)(2,1)S(1)} %bitcast.5, bf16[128,768]{1,0:T(8,128)(2,1)S(1)} %bitcast.7, ...), custom_call_target="tpu_custom_call" | custom-call | flops 603979776 | bytes 4000000 | tf_op jit(solution)/shard_map/pallas_call | solution.py:441
  71.7 0.6 reduce
  72.3 0.6 reduce.1
  72.9 0.7 copy.17
  73.7 0.6 copy.18
  74.3 0.6 copy.19
Async XLA Ops:
  2.7 1.7 %copy-start = (bf16[768,1536]{1,0:T(8,128)(2,1)S(1)}, bf16[768,1536]{1,0:T(8,128)(2,1)}, u32[]{:S(2)}) copy-start(bf16[768,1536]{1,0:T(8,128)(2,1)} %w_hbm.1) | copy-start | bytes 7077892
  4.3 1.0 %copy-start.1 = (bf16[1,128,1536]{2,1,0:T(8,128)(2,1)S(1)}, bf16[1,128,1536]{2,1,0:T(8,128)(2,1)}, u32[]{:S(2)}) copy-start(bf16[1,128,1536]{2,1,0:T(8,128)(2,1)} %param.8) | copy-start | bytes 1179652
  5.3 1.0 %copy-start.2 = (bf16[1,128,1536]{2,1,0:T(8,128)(2,1)S(1)}, bf16[1,128,1536]{2,1,0:T(8,128)(2,1)}, u32[]{:S(2)}) copy-start(bf16[1,128,1536]{2,1,0:T(8,128)(2,1)} %param.15) | copy-start | bytes 1179652
  6.3 0.9 %copy-start.3 = (bf16[1,128,768]{2,1,0:T(8,128)(2,1)S(1)}, bf16[1,128,768]{2,1,0:T(8,128)(2,1)}, u32[]{:S(2)}) copy-start(bf16[1,128,768]{2,1,0:T(8,128)(2,1)} %param.14) | copy-start | bytes 589828
  7.3 0.8 %copy-start.4 = (f32[5,1536]{1,0:T(8,128)S(1)}, f32[5,1536]{1,0:T(8,128)}, u32[]{:S(2)}) copy-start(f32[5,1536]{1,0:T(8,128)} %taps_ref.1) | copy-start | bytes 92164

commit v2 on v1

v2 whole, which is shorter than its diff:
```python
import functools

import jax
import jax.numpy as jnp
from jax import lax
from jax.experimental import pallas as pl
from jax.experimental.pallas import tpu as pltpu
from jax.sharding import PartitionSpec as P

STEP = 4
MESH = pl.DeviceIdType.MESH
BLOCK = 16
HALO = 8
XS = 4
LANES = 128
ROOT = 0.7978845608028654
CUBIC = 0.044715

LOC_X, LOC_COT, LOC_SKIP, LOC_W, LOC_OWN, LOC_ACT, LOC_LEN, LOC_TAPS, LOC_BIAS, LOC_GAIN, LOC_IG = range(11)
(S_HALO, S_COT, S_FWD, S_ACT, S_SIB, S_GRAD, S_EX, S_EY, S_EZ, S_EA, S_EF, S_PZ) = range(12)
(R_TOP, R_BOT, R_COTS, R_COT1, R_COT2, R_COT3, R_GTOP, R_GBOT, R_EX, R_EY, R_EZ, R_EA, R_EF, R_PZ) = range(14)
S_PY = 12
R_ACT, R_SIB, R_PY = 14, 23, 26
CHUNKS = 3
ORDER = (1, 0, 2)


def wait_bytes(ref, sem):
    pltpu.make_async_copy(ref, ref, sem).wait()


def kernel(
    ys,
    zs,
    len_hbm,
    x_hbm,
    cot_hbm,
    skip_hbm,
    w_hbm,
    taps_hbm,
    bias_hbm,
    gain_hbm,
    ig_ref,
    pg_ref,
    kg_ref,
    bg_ref,
    gg_ref,
    len_ref,
    taps_ref,
    bias_ref,
    gain_ref,
    x_v,
    cot_v,
    skip_v,
    w_v,
    back,
    halo_t,
    halo_b,
    xpad,
    gb,
    ig_v,
    ghalo_t,
    ghalo_b,
    gpad,
    eacc,
    cotg,
    cott,
    actc,
    actg,
    pacc,
    pbuf,
    yrecv,
    tbuf,
    zrecv,
    e_loc,
    e_x,
    e_1,
    e_y,
    e_z,
    e_fin,
    loc,
    snd,
    rcv,
    ysem,
    zsem,
):
    rows, chans = x_v.shape
    outs = cot_v.shape[1]
    half = outs // 2
    quarter = chans // XS
    taps = taps_ref.shape[0]
    samples = ys * zs
    own_rows = outs // samples
    yh, zh = ys // 2, zs // 2
    k_rows = own_rows * zh
    tile = tbuf.shape[2]
    e_rows = e_1.shape[1]

    dp = lax.axis_index("dp")
    s = lax.axis_index("seq")
    y, z = dp // zs, dp % zs
    x, c = s // 2, s % 2
    oc = 1 - c
    sib = 2 * x + oc

    def xat(delta, core):
        return (dp, 2 * ((x + delta) % XS) + core)

    def remote(src, dst, send, recv, device):
        return pltpu.make_async_remote_copy(
            src_ref=src, dst_ref=dst, send_sem=snd.at[send], recv_sem=rcv.at[recv], device_id=device, device_id_type=MESH
        )

    ld_x = pltpu.make_async_copy(x_hbm, x_v, loc.at[LOC_X])
    ld_cot = pltpu.make_async_copy(cot_hbm, cot_v, loc.at[LOC_COT])
    ld_w = pltpu.make_async_copy(w_hbm, w_v, loc.at[LOC_W])
    ld_skip = pltpu.make_async_copy(skip_hbm, skip_v, loc.at[LOC_SKIP])
    my_half = pl.multiple_of(c * half, LANES)
    ld_own = pltpu.make_async_copy(cot_hbm.at[:, pl.ds(my_half, half)], cotg.at[0], loc.at[LOC_OWN])
    ld_x.start()
    ld_cot.start()
    ld_w.start()
    ld_skip.start()
    ld_own.start()
    ld_len = pltpu.make_async_copy(len_hbm, len_ref, loc.at[LOC_LEN])
    ld_taps = pltpu.make_async_copy(taps_hbm, taps_ref, loc.at[LOC_TAPS])
    ld_bias = pltpu.make_async_copy(bias_hbm, bias_ref, loc.at[LOC_BIAS])
    ld_gain = pltpu.make_async_copy(gain_hbm, gain_ref, loc.at[LOC_GAIN])
    ld_len.start()
    ld_taps.start()
    ld_bias.start()
    ld_gain.start()

    barrier = pltpu.get_barrier_semaphore()
    for d in range(1, 2 * XS):
        pl.semaphore_signal(barrier, inc=1, device_id=(dp, (s + d) % (2 * XS)), device_id_type=MESH)
    y_steps = (1, ys - 1) if ys > 2 else (1,)
    z_steps = (1, zs - 1) if zs > 2 else (1,)
    for d in y_steps:
        for device in (s, sib):
            pl.semaphore_signal(barrier, inc=1, device_id=(((y + d) % ys) * zs + z, device), device_id_type=MESH)
    for d in z_steps:
        for device in (s, sib):
            pl.semaphore_signal(barrier, inc=1, device_id=(y * zs + (z + d) % zs, device), device_id_type=MESH)
    pl.semaphore_wait(barrier, 2 * XS - 1 + 2 * (1 if ys == 2 else 2) + 2 * (1 if zs == 2 else 2))

    reach_y = (1, 2) if ys == 8 else ()
    reach_z = (1, 2, 4) if zs == 16 else (1,) if zs == 4 else ()

    def tell(i):
        if i < len(reach_y):
            for d in (reach_y[i], ys - reach_y[i]):
                pl.semaphore_signal(ysem.at[i], inc=1, device_id=(((y + d) % ys) * zs + z, s), device_id_type=MESH)
        if i < len(reach_z):
            for d in (reach_z[i], zs - reach_z[i]):
                pl.semaphore_signal(zsem.at[i], inc=1, device_id=(y * zs + (z + d) % zs, s), device_id_type=MESH)

    def hear(i):
        if i < len(reach_y):
            pl.semaphore_wait(ysem.at[i], 2)
        if i < len(reach_z):
            pl.semaphore_wait(zsem.at[i], 2)

    up, down = (dp, (s + 1) % (2 * XS)), (dp, (s + 2 * XS - 1) % (2 * XS))
    remote(x_hbm.at[pl.ds(rows - BLOCK, BLOCK)], halo_t, S_HALO, R_TOP, up).start()
    remote(x_hbm.at[pl.ds(0, BLOCK)], halo_b, S_HALO, R_BOT, down).start()

    for delta, recv in ((1, R_COT3), (3, R_COT1), (0, R_COTS)):
        for p in (0, 1):
            if delta == 0 and p == 0:
                continue
            core = c if p == 0 else oc
            start = pl.multiple_of(core * half, LANES)
            remote(
                cot_hbm.at[:, pl.ds(start, half)], cotg.at[4 * p + (XS - delta) % XS], S_COT, recv, xat(delta, core)
            ).start()
    tell(0)

    ld_len.wait()
    length = len_ref[0]
    first = s * rows
    row_id = lax.broadcasted_iota(jnp.int32, (BLOCK, 1), 0)

    ld_cot.wait()
    ld_w.wait()
    ld_skip.wait()

    def back_step(i, carry):
        at = pl.ds(pl.multiple_of(i * quarter, LANES), quarter)
        back[:, at] = jnp.dot(cot_v[...], w_v[:, at], preferred_element_type=jnp.float32) + skip_v[:, at].astype(jnp.float32)
        return carry

    hear(0)
    tell(1)
    lax.fori_loop(0, XS, back_step, 0)

    ld_x.wait()
    ld_taps.wait()
    ld_bias.wait()
    ld_gain.wait()

    def mask_step(i, carry):
        r0 = pl.multiple_of(i * BLOCK, BLOCK)
        value = x_v[pl.ds(r0, BLOCK), :].astype(jnp.float32)
        xpad[pl.ds(r0 + HALO, BLOCK), :] = jnp.where(first + r0 + row_id < length, value, 0.0)
        return carry

    lax.fori_loop(0, rows // BLOCK, mask_step, 0)
    eacc[...] = jnp.zeros_like(eacc)

    wait_bytes(halo_t, rcv.at[R_TOP])
    wait_bytes(halo_b, rcv.at[R_BOT])
    head_id = first - HALO + lax.broadcasted_iota(jnp.int32, (HALO, 1), 0)
    head = halo_t[...].astype(jnp.float32)[BLOCK - HALO :]
    xpad[0:HALO, :] = jnp.where(jnp.logical_and(head_id >= 0, head_id < length), head, 0.0)
    tail_id = first + rows + lax.broadcasted_iota(jnp.int32, (HALO, 1), 0)
    tail = halo_b[...].astype(jnp.float32)[:HALO]
    xpad[pl.ds(rows + HALO, HALO), :] = jnp.where(
        jnp.logical_and(tail_id < length, s < 2 * XS - 1), tail, 0.0
    )

    def fold(value):
        return value[:HALO] + value[HALO:]

    def shifted(ref, r0):
        even = ref[pl.ds(r0, 2 * BLOCK), :]
        odd = even[STEP : STEP + BLOCK + HALO]
        return [even[:BLOCK], odd[:BLOCK], even[HALO : HALO + BLOCK], odd[HALO:], even[BLOCK:]]

    def main_step(i, carry):
        r0 = pl.multiple_of(i * BLOCK, BLOCK)
        seen = shifted(xpad, r0)
        hidden = bias_ref[...].reshape(1, chans) + taps_ref[0:1, :] * seen[0]
        for j in range(1, taps):
            hidden = hidden + taps_ref[j : j + 1, :] * seen[j]
        inverse = lax.rsqrt(jnp.mean(hidden * hidden, axis=-1, keepdims=True) + 1e-06)
        normed = hidden * inverse
        gain = gain_ref[...].reshape(1, chans)
        u = normed * gain
        square = u * u
        tanh = jnp.tanh(u * (ROOT + ROOT * CUBIC * square))
        cdf = 0.5 + 0.5 * tanh
        act = (u * cdf).astype(jnp.bfloat16)
        for m in range(XS * CHUNKS):
            actc[m, pl.ds(r0, BLOCK), :] = act[:, m * LANES : (m + 1) * LANES]
        slope = cdf + u * (1.0 - tanh * tanh) * (0.5 * ROOT + 1.5 * ROOT * CUBIC * square)
        toward = back[pl.ds(r0, BLOCK), :] * slope
        eacc[pl.ds((taps + 1) * HALO, HALO), :] += fold(toward * normed)
        toward = toward * gain
        pull = jnp.mean(toward * normed, axis=-1, keepdims=True)
        grad = ((toward - normed * pull) * inverse).astype(jnp.bfloat16)
        gb[pl.ds(r0, BLOCK), :] = grad
        grad = grad.astype(jnp.float32)
        gpad[pl.ds(r0 + HALO, BLOCK), :] = grad
        eacc[pl.ds(taps * HALO, HALO), :] += fold(grad)
        for j in range(taps):
            eacc[pl.ds(j * HALO, HALO), :] += fold(grad * seen[j])
        return carry

    lax.fori_loop(0, rows // BLOCK, main_step, 0)

    for r in range(taps + 2):
        line = jnp.sum(eacc[r * HALO : (r + 1) * HALO, :], axis=0, keepdims=True)
        for q in range(XS):
            e_loc[q, r : r + 1, :] = line[:, q * quarter : (q + 1) * quarter]
    for q in range(XS):
        e_loc[q, taps + 2 :, :] = jnp.zeros((HALO - taps - 2, quarter), jnp.float32)
    for delta in (2, 1, 3):
        remote(e_loc.at[(x + delta) % XS], e_x.at[XS - delta - 1], S_EX, R_EX, xat(delta, c)).start()

    remote(gb.at[pl.ds(rows - BLOCK, BLOCK)], ghalo_t, S_GRAD, R_GTOP, up).start()
    remote(gb.at[pl.ds(0, BLOCK)], ghalo_b, S_GRAD, R_GBOT, down).start()

    part = rows // 2
    wait_bytes(cotg.at[pl.ds(0, 2)], rcv.at[R_COT3])
    for p in (0, 1):
        at = pl.ds(0, part)
        remote(cotg.at[4 * p + 3, at], cotg.at[4 * p + 2, at], S_FWD, R_COT2, xat(1, c)).start()
    wait_bytes(cotg.at[pl.ds(0, 2)], rcv.at[R_COT1])
    for p in (0, 1):
        at = pl.ds(part, part)
        remote(cotg.at[4 * p + 1, at], cotg.at[4 * p + 2, at], S_FWD, R_COT2, xat(3, c)).start()

    for k in ORDER:
        for delta in (2, 1, 3):
            slot = XS - delta
            remote(
                actc.at[CHUNKS * ((x + delta) % XS) + k], actg.at[k, slot], S_ACT, R_ACT + 3 * k + slot - 1, xat(delta, c)
            ).start()
        remote(actc.at[CHUNKS * x + k], actg.at[k, 4], S_SIB, R_SIB + k, (dp, sib)).start()
        pltpu.make_async_copy(actc.at[CHUNKS * x + k], actg.at[k, 0], loc.at[LOC_ACT]).start()
    hear(1)
    tell(2)

    def turn(slot):
        cott[:, slot * rows : (slot + 1) * rows] = jnp.transpose(cotg[slot])

    ld_own.wait()
    wait_bytes(cotg.at[0], rcv.at[R_COTS])
    for slot in (0, 4, 1, 5, 3, 7):
        turn(slot)

    wait_bytes(ghalo_t, rcv.at[R_GTOP])
    wait_bytes(ghalo_b, rcv.at[R_GBOT])
    gpad[0:HALO, :] = jnp.where(s > 0, ghalo_t[...].astype(jnp.float32)[BLOCK - HALO :], 0.0)
    gpad[pl.ds(rows + HALO, HALO), :] = jnp.where(s < 2 * XS - 1, ghalo_b[...].astype(jnp.float32)[:HALO], 0.0)

    def input_step(i, carry):
        r0 = pl.multiple_of(i * BLOCK, BLOCK)
        seen = shifted(gpad, r0)
        total = taps_ref[0:1, :] * seen[taps - 1]
        for j in range(1, taps):
            total = total + taps_ref[j : j + 1, :] * seen[taps - 1 - j]
        ig_v[pl.ds(r0, BLOCK), :] = jnp.where(first + r0 + row_id < length, total, 0.0).astype(jnp.bfloat16)
        return carry

    lax.fori_loop(0, rows // BLOCK, input_step, 0)
    put_ig = pltpu.make_async_copy(ig_v, ig_ref, loc.at[LOC_IG])
    put_ig.start()
    hear(2)

    wait_bytes(e_x, rcv.at[R_EX])
    e_sum = e_loc[x] + e_x[0] + e_x[1] + e_x[2]
    for r in range(HALO):
        e_1[r // e_rows, r % e_rows : r % e_rows + 1, :] = e_sum[r : r + 1]
    for d in range(1, ys):
        other = (y + d) % ys
        remote(e_1.at[other], e_y.at[ys - d - 1], S_EY, R_EY, (other * zs + z, s)).start()

    wait_bytes(cotg.at[pl.ds(0, 2)], rcv.at[R_COT2])
    turn(2)
    turn(6)
    wait_bytes(actc.at[pl.ds(0, CHUNKS)], loc.at[LOC_ACT])

    def same_parity(k):
        for d in (1, 3, 2):
            wait_bytes(actg.at[k, d], rcv.at[R_ACT + 3 * k + d - 1])
            remote(actg.at[k, d], actg.at[k, 4 + d], S_SIB, R_SIB + k, (dp, sib)).start()
        pacc[k] = jnp.dot(
            cott[:, : 4 * rows], actg[k, 0:4].reshape(4 * rows, LANES), preferred_element_type=jnp.float32
        )

    def other_parity(k):
        wait_bytes(actg.at[k, pl.ds(4, 4)], rcv.at[R_SIB + k])
        whole = pacc[k] + jnp.dot(
            cott[:, 4 * rows :], actg[k, 4:8].reshape(4 * rows, LANES), preferred_element_type=jnp.float32
        )
        whole = whole.astype(jnp.bfloat16)
        for i in range(ys):
            pbuf[k, i] = whole[i * k_rows : (i + 1) * k_rows]
        for i in range(yh):
            for core in range(2):
                other = yh * c + i
                slot = (y + ys - other) % ys
                mine = jnp.logical_and(other == y, c == core)

                @pl.when(mine)
                def _():
                    yrecv[k, 0] = pbuf[k, 2 * i + core]

                @pl.when(jnp.logical_not(mine))
                def _():
                    remote(
                        pbuf.at[k, 2 * i + core], yrecv.at[k, slot], S_PY + k, R_PY + k, (other * zs + z, 2 * x + core)
                    ).start()

    same_parity(ORDER[0])
    same_parity(ORDER[1])
    other_parity(ORDER[0])
    same_parity(ORDER[2])
    other_parity(ORDER[1])
    other_parity(ORDER[2])

    wait_bytes(e_y, rcv.at[R_EY])
    e_row = e_1[y]
    for d in range(ys - 1):
        e_row = e_row + e_y[d]
    e_z[z] = e_row
    for d in range(1, zs):
        remote(e_z.at[z], e_z.at[z], S_EZ, R_EZ, (y * zs + (z + d) % zs, s)).start()

    own_y = y // yh == c
    sel_row = lax.broadcasted_iota(jnp.int32, (zh * tile, k_rows), 0)
    sel_col = lax.broadcasted_iota(jnp.int32, (zh * tile, k_rows), 1)
    within = sel_row % tile
    base = (sel_row // tile) * own_rows
    pick_a = jnp.logical_and(within < own_rows, sel_col == base + within).astype(jnp.bfloat16)
    low = within - tile // 2
    pick_b = jnp.logical_and(jnp.logical_and(low >= 0, low < own_rows), sel_col == base + low).astype(jnp.bfloat16)

    def over_y(k, pick):
        @pl.when(own_y)
        def _():
            wait_bytes(yrecv.at[k, pl.ds(0, ys - 1)], rcv.at[R_PY + k])

        @pl.when(jnp.logical_not(own_y))
        def _():
            wait_bytes(yrecv.at[k], rcv.at[R_PY + k])

        total = yrecv[k, 0].astype(jnp.float32)
        for d in range(1, ys):
            total = total + yrecv[k, d].astype(jnp.float32)
        return jnp.dot(pick, total.astype(jnp.bfloat16), preferred_element_type=jnp.float32)

    middle = over_y(1, pick_b)
    for q in range(2):
        both = (over_y(2 * q, pick_a) + middle).astype(jnp.bfloat16)
        for j in range(zh):
            tbuf[j, q] = both[j * tile : (j + 1) * tile]
        for j in range(zh):
            other = zh * c + j
            slot = (z + zs - other) % zs
            mine = jnp.logical_and(other == z, c == q)

            @pl.when(mine)
            def _():
                zrecv[0] = tbuf[j, q]

            @pl.when(jnp.logical_not(mine))
            def _():
                remote(tbuf.at[j, q], zrecv.at[slot], S_PZ, R_PZ, (y * zs + other, 2 * x + q)).start()

    wait_bytes(e_z.at[pl.ds(0, zs - 1)], rcv.at[R_EZ])
    e_row = e_z[0]
    for d in range(1, zs):
        e_row = e_row + e_z[d]
    e_fin[s, y] = e_row
    for d in range(1, ys):
        remote(e_fin.at[s, y], e_fin.at[s, y], S_EA, R_EA, (((y + d) % ys) * zs + z, s)).start()

    wait_bytes(e_fin.at[0, pl.ds(0, ys - 1)], rcv.at[R_EA])
    for d in range(1, 2 * XS):
        remote(e_fin.at[s], e_fin.at[s], S_EF, R_EF, (dp, (s + d) % (2 * XS))).start()

    own_z = z // zh == c

    @pl.when(own_z)
    def _():
        wait_bytes(zrecv.at[pl.ds(0, zs - 1)], rcv.at[R_PZ])

    @pl.when(jnp.logical_not(own_z))
    def _():
        wait_bytes(zrecv, rcv.at[R_PZ])

    final = zrecv[0].astype(jnp.float32)
    for d in range(1, zs):
        final = final + zrecv[d].astype(jnp.float32)
    final = final / samples
    side = final[:own_rows]
    inner = final[tile // 2 : tile // 2 + own_rows]
    cut = quarter // 2 - LANES
    first_half = jnp.concatenate([side, inner[:, :cut]], axis=1)
    second_half = jnp.concatenate([inner[:, cut:], side], axis=1)
    pg_ref[...] = jnp.where(c == 0, first_half, second_half)

    wait_bytes(e_fin.at[pl.ds(0, 2 * XS - 1)], rcv.at[R_EF])
    for q in range(XS):
        at = slice(q * quarter, (q + 1) * quarter)
        for r in range(taps + 2):
            line = (e_fin[2 * q, r // e_rows, r % e_rows : r % e_rows + 1] + e_fin[2 * q + 1, r // e_rows, r % e_rows : r % e_rows + 1]) / samples
            if r < taps:
                kg_ref[r : r + 1, at] = line
            elif r == taps:
                bg_ref[at] = line.reshape(quarter)
            else:
                gg_ref[at] = line.reshape(quarter)

    wait_bytes(x_v.at[pl.ds(0, 2 * BLOCK)], snd.at[S_HALO])
    wait_bytes(cotg.at[pl.ds(0, 5)], snd.at[S_COT])
    wait_bytes(cotg.at[pl.ds(0, 2)], snd.at[S_FWD])
    wait_bytes(actc.at[pl.ds(0, 9)], snd.at[S_ACT])
    wait_bytes(actc, snd.at[S_SIB])
    wait_bytes(gb.at[pl.ds(0, 2 * BLOCK)], snd.at[S_GRAD])
    wait_bytes(e_x, snd.at[S_EX])
    wait_bytes(e_y, snd.at[S_EY])
    wait_bytes(e_z.at[pl.ds(0, zs - 1)], snd.at[S_EZ])
    wait_bytes(e_fin.at[0, pl.ds(0, ys - 1)], snd.at[S_EA])
    wait_bytes(e_fin.at[pl.ds(0, 2 * XS - 1)], snd.at[S_EF])

    @pl.when(own_y)
    def _():
        for k in range(CHUNKS):
            wait_bytes(pbuf.at[k, pl.ds(0, ys - 1)], snd.at[S_PY + k])

    @pl.when(jnp.logical_not(own_y))
    def _():
        for k in range(CHUNKS):
            wait_bytes(pbuf.at[k], snd.at[S_PY + k])
    put_ig.wait()

    @pl.when(own_z)
    def _():
        wait_bytes(zrecv.at[pl.ds(0, zs - 1)], snd.at[S_PZ])

    @pl.when(jnp.logical_not(own_z))
    def _():
        wait_bytes(zrecv, snd.at[S_PZ])


def put_kernel(ig_in, pg_in, kg_in, bg_in, gg_in, ig_out, pg_out, kg_out, bg_out, gg_out):
    ig_out[...] = ig_in[...]
    pg_out[...] = pg_in[...]
    kg_out[...] = kg_in[...]
    bg_out[...] = bg_in[...]
    gg_out[...] = gg_in[...]


def shards(ys, zs, section, lengths, taps, bias, gain, weight, cot, skip):
    samp, rows, chans = section.shape
    outs = cot.shape[2]
    half, quarter = outs // 2, chans // XS
    samples = ys * zs
    own_rows = outs // samples
    k_rows = own_rows * (zs // 2)
    tile = 2 * (-(-own_rows // 8) * 8)
    e_rows = HALO // ys
    kinds = taps.shape[0]
    bf16, f32 = jnp.bfloat16, jnp.float32
    vmem = pl.BlockSpec(memory_space=pltpu.VMEM)
    hbm = pl.BlockSpec(memory_space=pl.ANY)
    shapes = (
        jax.ShapeDtypeStruct((rows, chans), bf16),
        jax.ShapeDtypeStruct((own_rows, quarter // 2), f32),
        jax.ShapeDtypeStruct((kinds, chans), f32),
        jax.ShapeDtypeStruct((chans,), f32),
        jax.ShapeDtypeStruct((chans,), f32),
    )
    result = pl.pallas_call(
        functools.partial(kernel, ys, zs),
        out_shape=shapes,
        in_specs=[hbm] * 8,
        out_specs=(hbm,) + (vmem,) * 4,
        scratch_shapes=[
            pltpu.SMEM((samp,), jnp.int32),
            pltpu.VMEM((kinds, chans), f32),
            pltpu.VMEM((chans,), f32),
            pltpu.VMEM((chans,), f32),
            pltpu.VMEM((rows, chans), bf16),
            pltpu.VMEM((rows, outs), bf16),
            pltpu.VMEM((rows, chans), bf16),
            pltpu.VMEM((outs, chans), bf16),
            pltpu.VMEM((rows, chans), f32),
            pltpu.VMEM((BLOCK, chans), bf16),
            pltpu.VMEM((BLOCK, chans), bf16),
            pltpu.VMEM((rows + 2 * HALO, chans), f32),
            pltpu.VMEM((rows, chans), bf16),
            pltpu.VMEM((rows, chans), bf16),
            pltpu.VMEM((BLOCK, chans), bf16),
            pltpu.VMEM((BLOCK, chans), bf16),
            pltpu.VMEM((rows + 2 * HALO, chans), f32),
            pltpu.VMEM(((kinds + 2) * HALO, chans), f32),
            pltpu.VMEM((8, rows, half), bf16),
            pltpu.VMEM((half, 8 * rows), bf16),
            pltpu.VMEM((XS * CHUNKS, rows, LANES), bf16),
            pltpu.VMEM((CHUNKS, 8, rows, LANES), bf16),
            pltpu.VMEM((CHUNKS, half, LANES), f32),
            pltpu.VMEM((CHUNKS, ys, k_rows, LANES), bf16),
            pltpu.VMEM((CHUNKS, ys, k_rows, LANES), bf16),
            pltpu.VMEM((zs // 2, 2, tile, LANES), bf16),
            pltpu.VMEM((zs, tile, LANES), bf16),
            pltpu.VMEM((XS, HALO, quarter), f32),
            pltpu.VMEM((XS - 1, HALO, quarter), f32),
            pltpu.VMEM((ys, e_rows, quarter), f32),
            pltpu.VMEM((ys - 1, e_rows, quarter), f32),
            pltpu.VMEM((zs, e_rows, quarter), f32),
            pltpu.VMEM((2 * XS, ys, e_rows, quarter), f32),
            pltpu.SemaphoreType.DMA((11,)),
            pltpu.SemaphoreType.DMA((15,)),
            pltpu.SemaphoreType.DMA((29,)),
            pltpu.SemaphoreType.REGULAR((2,)),
            pltpu.SemaphoreType.REGULAR((3,)),
        ],
        compiler_params=pltpu.CompilerParams(collective_id=0, has_side_effects=True, vmem_limit_bytes=56 * 1024 * 1024),
        cost_estimate=pl.CostEstimate(flops=4 * rows * outs * chans, bytes_accessed=4_000_000, transcendentals=rows * chans),
    )(
        lengths,
        section.reshape(rows, chans),
        cot.reshape(rows, outs),
        skip.reshape(rows, chans),
        weight,
        taps,
        bias,
        gain,
    )
    result = pl.pallas_call(
        put_kernel,
        out_shape=shapes,
        in_specs=[vmem] * 5,
        out_specs=(vmem,) * 5,
        compiler_params=pltpu.CompilerParams(vmem_limit_bytes=56 * 1024 * 1024),
    )(result[0], result[1], result[2], result[3], result[4])
    return result[0].reshape(section.shape), result[1], result[2], result[3], result[4]


def solution(mesh):
    dp = mesh.shape["dp"]
    ys = 8 if dp == 128 else 2
    in_specs = (
        P("dp", "seq", None),
        P("dp"),
        P(),
        P(),
        P(),
        P(),
        P("dp", "seq", None),
        P("dp", "seq", None),
    )
    out_specs = (P("dp", "seq", None), P("dp", "seq"), P(), P(), P())
    return jax.shard_map(
        functools.partial(shards, ys, dp // ys), mesh=mesh, in_specs=in_specs, out_specs=out_specs, check_vma=False
    )
```

time: 75.3 us -> 60.1 us (0.80)
  the two profiles are of different devices: /device:TPU:9 before, /device:TPU:1 now
where the time goes in v2:
time: 60.1 us; the launch traced here: 60 us
  Pallas kernels  58.7 us (98%)
  between operations  1.29 us (2%)
    pallas_call x1, Pallas kernels, shards(): pl.pallas_call(functools.partial(kernel, ys, zs), out_shape=shapes, in_sp...  56.8 us
    pallas_call x1, Pallas kernels, shards(): pl.pallas_call(put_kernel, out_shape=shapes, in_specs=[vmem] * 5, out_spe...  1.82 us

profile of v2, /device:TPU:1, one launch (start us, length us, event | category | flops | bytes accessed | tf_op | source)
XLA Modules:
  0.0 60.0 jit_solution(2312020393796761708)
XLA Ops:
  1.3 56.8 %shard_map.119 = (bf16[128,1536]{1,0:T(8,128)(2,1)}, f32[6,192]{1,0:T(8,128)}, f32[5,1536]{1,0:T(8,128)}, f32[1536]{0:T(1024)}, f32[1536]{0:T(1024)}) custom-call(s32[1]{0:T(128)S(6)} %copy.13.len_hbm, bf16[128,1536]{1,0:T(8,128)(2,1)} %bitcast.4, bf16[128,768]{1,0:T(8,128)(2,1)} %bitcast.6, bf16[128,1536]{1,0:T(8,128)(2,1)} %bitcast.5, ...), custom_call_target="tpu_custom_call" | custom-call | flops 603979776 | bytes 4000000 | tf_op jit(solution)/shard_map/pallas_call | solution.py:528
  58.1 1.8 %shard_map.120 = (bf16[128,1536]{1,0:T(8,128)(2,1)}, f32[6,192]{1,0:T(8,128)}, f32[5,1536]{1,0:T(8,128)}, f32[1536]{0:T(1024)}, f32[1536]{0:T(1024)}) custom-call(bf16[128,1536]{1,0:T(8,128)(2,1)} %get-tuple-element.15.ig_in, f32[6,192]{1,0:T(8,128)} %get-tuple-element.16.pg_in, f32[5,1536]{1,0:T(8,128)} %get-tuple-element.17.kg_in, ...), custom_call_target="tpu_custom_call" | custom-call | tf_op jit(solution)/shard_map/pallas_call | solution.py:585

commit v3 on v2

--- a/solution.py
+++ b/solution.py
@@ -350,34 +350,51 @@
             pbuf[k, i] = whole[i * k_rows : (i + 1) * k_rows]
         for i in range(yh):
             for core in range(2):
-                other = yh * c + i
+                turn_i = (y + i) % yh
+                other = yh * c + turn_i
                 slot = (y + ys - other) % ys
                 mine = jnp.logical_and(other == y, c == core)
 
                 @pl.when(mine)
                 def _():
-                    yrecv[k, 0] = pbuf[k, 2 * i + core]
+                    yrecv[k, 0] = pbuf[k, 2 * turn_i + core]
 
                 @pl.when(jnp.logical_not(mine))
                 def _():
                     remote(
-                        pbuf.at[k, 2 * i + core], yrecv.at[k, slot], S_PY + k, R_PY + k, (other * zs + z, 2 * x + core)
+                        pbuf.at[k, 2 * turn_i + core], yrecv.at[k, slot], S_PY + k, R_PY + k, (other * zs + z, 2 * x + core)
                     ).start()
 
+    def small_over_y():
+        wait_bytes(e_y, rcv.at[R_EY])
+        e_row = e_1[y]
+        for d in range(ys - 1):
+            e_row = e_row + e_y[d]
+        e_z[z] = e_row
+        for d in range(1, zs):
+            remote(e_z.at[z], e_z.at[z], S_EZ, R_EZ, (y * zs + (z + d) % zs, s)).start()
+
+    def small_over_z():
+        wait_bytes(e_z.at[pl.ds(0, zs - 1)], rcv.at[R_EZ])
+        e_row = e_z[0]
+        for d in range(1, zs):
+            e_row = e_row + e_z[d]
+        e_fin[s, y] = e_row
+        for d in range(1, ys):
+            remote(e_fin.at[s, y], e_fin.at[s, y], S_EA, R_EA, (((y + d) % ys) * zs + z, s)).start()
+
+    def small_to_all():
+        wait_bytes(e_fin.at[0, pl.ds(0, ys - 1)], rcv.at[R_EA])
+        for d in range(1, 2 * XS):
+            remote(e_fin.at[s], e_fin.at[s], S_EF, R_EF, (dp, (s + d) % (2 * XS))).start()
+
     same_parity(ORDER[0])
+    small_over_y()
     same_parity(ORDER[1])
     other_parity(ORDER[0])
     same_parity(ORDER[2])
     other_parity(ORDER[1])
     other_parity(ORDER[2])
-
-    wait_bytes(e_y, rcv.at[R_EY])
-    e_row = e_1[y]
-    for d in range(ys - 1):
-        e_row = e_row + e_y[d]
-    e_z[z] = e_row
-    for d in range(1, zs):
-        remote(e_z.at[z], e_z.at[z], S_EZ, R_EZ, (y * zs + (z + d) % zs, s)).start()
 
     own_y = y // yh == c
     sel_row = lax.broadcasted_iota(jnp.int32, (zh * tile, k_rows), 0)
@@ -402,56 +419,27 @@
             total = total + yrecv[k, d].astype(jnp.float32)
         return jnp.dot(pick, total.astype(jnp.bfloat16), preferred_element_type=jnp.float32)
 
+    small_over_z()
     middle = over_y(1, pick_b)
     for q in range(2):
+        if q == 1:
+            small_to_all()
         both = (over_y(2 * q, pick_a) + middle).astype(jnp.bfloat16)
         for j in range(zh):
             tbuf[j, q] = both[j * tile : (j + 1) * tile]
         for j in range(zh):
-            other = zh * c + j
+            turn_j = (z + j) % zh
+            other = zh * c + turn_j
             slot = (z + zs - other) % zs
             mine = jnp.logical_and(other == z, c == q)
 
             @pl.when(mine)
             def _():
-                zrecv[0] = tbuf[j, q]
+                zrecv[0] = tbuf[turn_j, q]
 
             @pl.when(jnp.logical_not(mine))
             def _():
-                remote(tbuf.at[j, q], zrecv.at[slot], S_PZ, R_PZ, (y * zs + other, 2 * x + q)).start()
-
-    wait_bytes(e_z.at[pl.ds(0, zs - 1)], rcv.at[R_EZ])
-    e_row = e_z[0]
-    for d in range(1, zs):
-        e_row = e_row + e_z[d]
-    e_fin[s, y] = e_row
-    for d in range(1, ys):
-        remote(e_fin.at[s, y], e_fin.at[s, y], S_EA, R_EA, (((y + d) % ys) * zs + z, s)).start()
-
-    wait_bytes(e_fin.at[0, pl.ds(0, ys - 1)], rcv.at[R_EA])
-    for d in range(1, 2 * XS):
-        remote(e_fin.at[s], e_fin.at[s], S_EF, R_EF, (dp, (s + d) % (2 * XS))).start()
-
-    own_z = z // zh == c
-
-    @pl.when(own_z)
-    def _():
-        wait_bytes(zrecv.at[pl.ds(0, zs - 1)], rcv.at[R_PZ])
-
-    @pl.when(jnp.logical_not(own_z))
-    def _():
-        wait_bytes(zrecv, rcv.at[R_PZ])
-
-    final = zrecv[0].astype(jnp.float32)
-    for d in range(1, zs):
-        final = final + zrecv[d].astype(jnp.float32)
-    final = final / samples
-    side = final[:own_rows]
-    inner = final[tile // 2 : tile // 2 + own_rows]
-    cut = quarter // 2 - LANES
-    first_half = jnp.concatenate([side, inner[:, :cut]], axis=1)
-    second_half = jnp.concatenate([inner[:, cut:], side], axis=1)
-    pg_ref[...] = jnp.where(c == 0, first_half, second_half)
+                remote(tbuf.at[turn_j, q], zrecv.at[slot], S_PZ, R_PZ, (y * zs + other, 2 * x + q)).start()
 
     wait_bytes(e_fin.at[pl.ds(0, 2 * XS - 1)], rcv.at[R_EF])
     for q in range(XS):
@@ -464,6 +452,27 @@
                 bg_ref[at] = line.reshape(quarter)
             else:
                 gg_ref[at] = line.reshape(quarter)
+
+    own_z = z // zh == c
+
+    @pl.when(own_z)
+    def _():
+        wait_bytes(zrecv.at[pl.ds(0, zs - 1)], rcv.at[R_PZ])
+
+    @pl.when(jnp.logical_not(own_z))
+    def _():
+        wait_bytes(zrecv, rcv.at[R_PZ])
+
+    final = zrecv[0].astype(jnp.float32)
+    for d in range(1, zs):
+        final = final + zrecv[d].astype(jnp.float32)
+    final = final / samples
+    side = final[:own_rows]
+    inner = final[tile // 2 : tile // 2 + own_rows]
+    cut = quarter // 2 - LANES
+    first_half = jnp.concatenate([side, inner[:, :cut]], axis=1)
+    second_half = jnp.concatenate([inner[:, cut:], side], axis=1)
+    pg_ref[...] = jnp.where(c == 0, first_half, second_half)
 
     wait_bytes(x_v.at[pl.ds(0, 2 * BLOCK)], snd.at[S_HALO])
     wait_bytes(cotg.at[pl.ds(0, 5)], snd.at[S_COT])

time: 60.1 us -> 58.8 us (0.978)
  Pallas kernels: 58.7 us -> 57.4 us
    pallas_call x1, Pallas kernels: 56.8 us -> 55.5 us  [shards(): pl.pallas_call(functools.partial(kernel, ys, zs), out_shape=shapes, in_sp...]
where the time goes in v3:
time: 58.8 us; the launch traced here: 58.6 us
  Pallas kernels  57.4 us (98%)
  between operations  1.29 us (2%)
    pallas_call x1, Pallas kernels, shards(): pl.pallas_call(functools.partial(kernel, ys, zs), out_shape=shapes, in_sp...  55.5 us
    pallas_call x1, Pallas kernels, shards(): pl.pallas_call(put_kernel, out_shape=shapes, in_specs=[vmem] * 5, out_spe...  1.82 us

profile of v3, /device:TPU:1, one launch (start us, length us, event | category | flops | bytes accessed | tf_op | source)
XLA Modules:
  0.0 58.6 jit_solution(8635361883735743495)
XLA Ops:
  1.3 55.5 %shard_map.119 = (bf16[128,1536]{1,0:T(8,128)(2,1)}, f32[6,192]{1,0:T(8,128)}, f32[5,1536]{1,0:T(8,128)}, f32[1536]{0:T(1024)}, f32[1536]{0:T(1024)}) custom-call(s32[1]{0:T(128)S(6)} %copy.13.len_hbm, bf16[128,1536]{1,0:T(8,128)(2,1)} %bitcast.4, bf16[128,768]{1,0:T(8,128)(2,1)} %bitcast.6, bf16[128,1536]{1,0:T(8,128)(2,1)} %bitcast.5, ...), custom_call_target="tpu_custom_call" | custom-call | flops 603979776 | bytes 4000000 | tf_op jit(solution)/shard_map/pallas_call | solution.py:537
  56.8 1.8 %shard_map.120 = (bf16[128,1536]{1,0:T(8,128)(2,1)}, f32[6,192]{1,0:T(8,128)}, f32[5,1536]{1,0:T(8,128)}, f32[1536]{0:T(1024)}, f32[1536]{0:T(1024)}) custom-call(bf16[128,1536]{1,0:T(8,128)(2,1)} %get-tuple-element.15.ig_in, f32[6,192]{1,0:T(8,128)} %get-tuple-element.16.pg_in, f32[5,1536]{1,0:T(8,128)} %get-tuple-element.17.kg_in, ...), custom_call_target="tpu_custom_call" | custom-call | tf_op jit(solution)/shard_map/pallas_call | solution.py:594
